TPU v7x, 32 devices: a whole 2x2x4 slice. The times are simulated.
32 devices in a mesh: frag: 2 (over y), pair: 4 (over z), occ: 4 (over x, core).
Axes of the slice: x: 2, y: 2, z: 4, core: 2. Of those that a mesh axis runs over, the one named last changes fastest.
Arguments:
- quarter_integrals: bfloat16 [24, 12, 128, 128], P(('frag', 'occ'), 'pair'), parts along dimension 0, may hold values from -6 to 6
- occ_coef: bfloat16 [2560, 1536], P('frag', 'occ'), parts along dimension 0, may hold values from -0.5 to 0.5
- vir_coef: bfloat16 [2560, 4096], P('frag', 'occ'), parts along dimension 0, may hold values from -0.15625 to 0.15625
- screened_block_mask: int32 [20, 10], P('frag'), parts along dimension 0, may hold values from 0 to 1, as said below
- tile_holder_pair: int32 [20, 10], P('frag'), parts along dimension 0, may hold values from 0 to 3, as said below
- shell_size: int32 [20], P('frag'), parts along dimension 0, may hold values from 64 to 128
Outputs:
- mo_block: bfloat16 [24, 1536, 4096], P('frag', 'pair', 'occ'), parts along dimension 0
There are 2 independent parts, one for each index of `frag`. A program takes and returns all parts, laid end to end along the dimension named above; each array names one. Nothing has to cross between parts.
Inputs may be any that keep to these rules, and one draw needn't show every extreme that they name: screened_block_mask is 1 for the shell-block pairs kept by the screening. At most 3 kept pairs have the same tile_holder_pair, and some pair index owns exactly 3. For a kept pair, tile_holder_pair is the pair index whose slots hold its tile; for other pairs it has no meaning.
All inputs are finite; a program needn't handle non-finite values.
Results may differ from a plain program's by a relative error of at most 0.0057.
Values may be sent and summed in bfloat16 or wider, within the bound.
A program may use at most 64 MiB of HBM per device.

v0:
```python
import jax
import jax.numpy as jnp
from jax import lax
from jax.sharding import PartitionSpec as P


def slot_lookup_table(screened_block_mask, tile_holder_pair, slot_count, tile_slots):
    block_count = screened_block_mask.shape[0]
    kept_tiles = screened_block_mask.reshape(-1)
    owners = tile_holder_pair.reshape(-1)
    tile_index = jnp.arange(kept_tiles.shape[0], dtype=jnp.int32)
    earlier = (
        (owners[:, None] == owners[None, :])
        & (tile_index[None, :] < tile_index[:, None])
        & (kept_tiles[None, :] == 1)
    )
    rank_within = jnp.sum(earlier.astype(jnp.int32), axis=1)
    slot_of = owners * tile_slots + rank_within
    slot_index = jnp.arange(slot_count, dtype=jnp.int32)
    holding = ((slot_of[None, :] == slot_index[:, None]) & (kept_tiles[None, :] == 1)).astype(
        jnp.int32
    )
    slot_occupied_flag = jnp.sum(holding, axis=1)
    slot_lambda_block = jnp.sum(holding * (tile_index // block_count)[None, :], axis=1)
    slot_sigma_block = jnp.sum(holding * (tile_index % block_count)[None, :], axis=1)
    return (slot_occupied_flag, slot_lambda_block, slot_sigma_block)


def trim_rows(coefficients, shell_size, slot_width):
    inside = jnp.arange(slot_width, dtype=jnp.int32)[None, :] < shell_size[:, None]
    return jnp.where(inside.reshape(-1)[:, None], coefficients, jnp.zeros((), coefficients.dtype))


def spread_tiles(placing, tile_parts):
    spread = jnp.einsum("kn,krjs->rjns", placing, tile_parts, preferred_element_type=jnp.float32)
    return spread.reshape(spread.shape[0], spread.shape[1], -1)


def per_device(
    quarter_integrals, occ_coef, vir_coef, screened_block_mask, tile_holder_pair, shell_size
):
    block_count = screened_block_mask.shape[0]
    slot_width = quarter_integrals.shape[3]
    tile_slots = quarter_integrals.shape[1]
    pair_count = lax.axis_size("pair")
    pair_index = lax.axis_index("pair")
    shard_width = occ_coef.shape[1]
    occ_total = shard_width * lax.axis_size("occ")
    slot_occupied_flag, slot_lambda_block, slot_sigma_block = slot_lookup_table(
        screened_block_mask, tile_holder_pair, pair_count * tile_slots, tile_slots
    )
    occ_used = trim_rows(occ_coef, shell_size, slot_width)
    vir_used = trim_rows(vir_coef, shell_size, slot_width)
    block_ids = jnp.arange(block_count, dtype=jnp.int32)
    placing = (
        (slot_sigma_block[:, None] == block_ids[None, :]) & (slot_occupied_flag[:, None] > 0)
    ).astype(jnp.bfloat16)
    own_lam = lax.dynamic_slice_in_dim(slot_lambda_block, pair_index * tile_slots, tile_slots)
    panel_whole = lax.all_gather(occ_used, "occ", axis=1, tiled=True)
    panel_rows = panel_whole.reshape(block_count, slot_width, occ_total)[own_lam]
    tile_parts = jnp.einsum(
        "rkls,klj->krjs", quarter_integrals, panel_rows, preferred_element_type=jnp.float32
    ).astype(jnp.bfloat16)
    summed = spread_tiles(
        placing, lax.all_to_all(tile_parts, "pair", split_axis=2, concat_axis=0, tiled=True)
    )
    half_mo = summed.astype(jnp.bfloat16)
    return jnp.einsum(
        "rjs,sb->rjb",
        lax.all_gather(half_mo, "occ", axis=0, tiled=True),
        vir_used,
        preferred_element_type=jnp.float32,
    ).astype(jnp.bfloat16)


def solution(mesh):
    placed = (
        P(("frag", "occ"), "pair", None, None),
        P("frag", "occ"),
        P("frag", "occ"),
        P("frag", None),
        P("frag", None),
        P("frag"),
    )
    return jax.shard_map(
        per_device, mesh=mesh, in_specs=placed, out_specs=P("frag", "pair", "occ"), check_vma=False
    )
```

profile of v0, /device:TPU:29, one launch (start us, length us, event | category | flops | bytes accessed | tf_op | source)
XLA Modules:
  0.0 294.9 jit_solution(14259401199756082072)
XLA Ops:
  6.5 0.0 copy-start
  6.5 0.0 all-gather.3.cloned.1.call-start
  6.5 0.8 fusion.13
  7.3 2.4 broadcast_select_fusion
  9.7 0.0 all-gather.3.cloned.1.call-update
  9.7 0.8 reshape.67
  10.5 0.7 broadcast_compare_fusion
  11.2 0.1 eq.57
  11.3 0.2 convert_reduce_fusion
  11.5 0.2 convert_reduce_fusion.1
  11.7 0.1 compare_select_fusion
  11.8 32.4 %all-gather.3.cloned.1.call-done = bf16[1280,1536]{1,0:T(8,128)(2,1)} async-done(((bf16[1280,384]{1,0:T(8,128)(2,1)}), bf16[1280,1536]{1,0:T(8,128)(2,1)}) %all-gather.3.cloned.1.call-update) | async-done | bytes 3932176 | tf_op jit(solution)/shard_map/all_gather | solution.py:59
  44.2 2.7 gather_fusion
  46.9 0.0 copy-done
  46.9 1.1 fusion.2
  48.1 17.6 %copy.31 = bf16[3,3,1536,128]{3,1,0,2:T(4,128)(2,1)} copy(bf16[3,3,1536,128]{3,2,1,0:T(8,128)(2,1)S(1)} %fusion.2) | data formatting | bytes 7077888 | tf_op jit(solution)/shard_map/convert_element_type | solution.py:63
  65.6 5.1 %all-to-all-start = ((bf16[3,3,1536,128]{3,1,0,2:T(4,128)(2,1)}), bf16[3,3,1536,128]{3,1,0,2:T(4,128)(2,1)}, u32[]{:S(2)}, u32[]{:S(2)}) async-start(bf16[3,3,1536,128]{3,1,0,2:T(4,128)(2,1)} %copy.31), calls=%async_computation | async-start | bytes 9437184 | tf_op jit(solution)/shard_map/all_to_all | solution.py:65
  70.7 0.0 all-gather.5.cloned.1.call-start
  70.8 102.2 %all-to-all-done = bf16[3,3,1536,128]{3,1,0,2:T(4,128)(2,1)} async-done(((bf16[3,3,1536,128]{3,1,0,2:T(4,128)(2,1)}), bf16[3,3,1536,128]{3,1,0,2:T(4,128)(2,1)}, u32[]{:S(2)}, u32[]{:S(2)}) %all-to-all-start) | async-done | bytes 3538976 | tf_op jit(solution)/shard_map/all_to_all | solution.py:65
  173.0 2.8 copy.32
  175.8 0.4 copy.33
  176.2 4.7 %convert_bitcast_fusion = bf16[3,384,10,128]{3,2,1,0:T(8,128)(2,1)} fusion(bf16[12,3,384,128]{3,2,1,0:T(8,128)(2,1)S(1)} %bitcast.26, s32[12]{0:T(128)S(1)} %get-tuple-element.6, pred[12]{0:T(512)(128)(4,1)S(1)} %broadcast_compare_fusion.1), kind=kOutput, calls=%fused_computation.4 | convolution fusion | flops 36864240 | bytes 6488124 | tf_op jit(solution)/shard_map/kn,krjs->rjns/dot_general | solution.py:35
  180.9 6.3 %copy.35 = bf16[3,384,10,128]{1,3,2,0:T(8,128)(2,1)S(1)} copy(bf16[3,384,10,128]{3,2,1,0:T(8,128)(2,1)} %convert_bitcast_fusion) | data formatting | bytes 5898240 | tf_op jit(solution)/shard_map/convert_element_type | solution.py:67
  187.2 3.4 %copy.36 = bf16[3,384,1280]{2,1,0:T(8,128)(2,1)} copy(bf16[3,384,1280]{1,2,0:T(8,128)(2,1)S(1)} %bitcast.28) | data formatting | bytes 5898240 | tf_op jit(solution)/shard_map/convert_element_type | solution.py:67
  190.6 0.0 all-gather.5.cloned.1.call-update
  190.6 78.6 %all-gather.5.cloned.1.call-done = bf16[12,384,1280]{2,1,0:T(8,128)(2,1)} async-done(((bf16[3,384,1280]{2,1,0:T(8,128)(2,1)}), bf16[12,384,1280]{2,1,0:T(8,128)(2,1)}) %all-gather.5.cloned.1.call-update) | async-done | bytes 11796496 | tf_op jit(solution)/shard_map/all_gather | solution.py:70
  269.2 18.8 %convolution_convert_fusion = bf16[12,384,1024]{2,1,0:T(8,128)(2,1)} fusion(bf16[12,384,1280]{2,1,0:T(8,128)(2,1)} %all-gather.5.cloned.1.call-done, bf16[1280,1024]{1,0:T(8,128)(2,1)} %param.8, pred[1280]{0:T(1024)(128)(4,1)S(1)} %fusion.13), kind=kOutput, calls=%fused_computation.1 | convolution fusion | flops 12085624832 | bytes 23856384 | tf_op jit(solution)/shard_map/rjs,sb->rjb/dot_general | solution.py:68
  (4 shorter events, 0.0 us)
Async XLA Ops:
  6.5 40.4 %copy-start = (bf16[3,3,128,128]{3,2,1,0:T(8,128)(2,1)S(1)}, bf16[3,3,128,128]{3,2,1,0:T(8,128)(2,1)}, u32[]{:S(2)}) copy-start(bf16[3,3,128,128]{3,2,1,0:T(8,128)(2,1)} %param.6) | copy-start | bytes 884740
  6.5 37.6 %all-gather.3.cloned.1.call-start = ((), (), s32[]{:S(2)}) async-start(), calls=%async_computation.1 | async-start | bytes 4915200 | tf_op jit(solution)/shard_map/all_gather | solution.py:59
  65.6 107.4 %all-to-all-start = ((bf16[3,3,1536,128]{3,1,0,2:T(4,128)(2,1)}), bf16[3,3,1536,128]{3,1,0,2:T(4,128)(2,1)}, u32[]{:S(2)}, u32[]{:S(2)}) async-start(bf16[3,3,1536,128]{3,1,0,2:T(4,128)(2,1)} %copy.31), calls=%async_computation | async-start | bytes 9437184 | tf_op jit(solution)/shard_map/all_to_all | solution.py:65
  70.7 198.5 %all-gather.5.cloned.1.call-start = ((), (), s32[]{:S(2)}) async-start(), calls=%async_computation.2 | async-start | bytes 14745600 | tf_op jit(solution)/shard_map/all_gather | solution.py:70
Sparse Core Ops, SparseCore 0:
  9.8 34.2 all-gather.2
  190.7 78.4 all-gather.4
where the time goes:
time: 297 us; the launch traced here: 295 us
  waiting for transfers between devices  213 us (72%)
  local copies, waits for them, and re-layouts  34.1 us (11%)
  matrix products  24.7 us (8%)
  between operations  13.5 us (5%)
  starting transfers between devices  5.14 us (2%)
  other arithmetic  4.31 us (1%)
    all_to_all x1, waiting for transfers between devices, per_device(): lax.all_to_all(tile_parts, 'pair', split_axis=2, concat_axis=0, tiled=True)  102 us
    all_gather x1, waiting for transfers between devices, per_device(): lax.all_gather(half_mo, 'occ', axis=0, tiled=True)  78.6 us
    all_gather x1, waiting for transfers between devices, per_device(): panel_whole = lax.all_gather(occ_used, 'occ', axis=1, tiled=True)  32.4 us
    dot_general x1, matrix products, per_device(): jnp.einsum('rjs,sb->rjb', lax.all_gather(half_mo, 'occ', axis=0, tiled=Tr...  18.8 us
    convert_element_type x1, local copies, waits for them, and re-layouts, per_device(): tile_parts = jnp.einsum('rkls,klj->krjs', quarter_integrals, panel_rows,...  17.6 us
    convert_element_type x2, local copies, waits for them, and re-layouts, per_device(): half_mo = summed.astype(jnp.bfloat16)  9.66 us
  transfers between devices with their start and end apart: 3, of which 3 were waited for; matrix products, arithmetic and copies ran while one was open for 1% of the time, Pallas kernels for 0%

commit v1 on v0

--- a/solution.py
+++ b/solution.py
@@ -1,6 +1,10 @@
+import functools
+
 import jax
 import jax.numpy as jnp
 from jax import lax
+from jax.experimental import pallas as pl
+from jax.experimental.pallas import tpu as pltpu
 from jax.sharding import PartitionSpec as P
 
 
@@ -36,7 +40,7 @@
     return spread.reshape(spread.shape[0], spread.shape[1], -1)
 
 
-def per_device(
+def send_tiles(
     quarter_integrals, occ_coef, vir_coef, screened_block_mask, tile_holder_pair, shell_size
 ):
     block_count = screened_block_mask.shape[0]
@@ -73,6 +77,129 @@
     ).astype(jnp.bfloat16)
 
 
+def transform_kernel(
+    lam_ref, rank_ref, used_ref, pairs_ref, integrals_ref, panel_ref, vir_ref, out_ref, half_ref
+):
+    n_pair, _, tile_slots, width, _ = integrals_ref.shape[1:]
+    half_ref[...] = jnp.zeros_like(half_ref)
+    for p in range(n_pair):
+        for k in range(tile_slots):
+            t = p * tile_slots + k
+
+            @pl.when(used_ref[t] > 0)
+            def _():
+                lam = pl.multiple_of(lam_ref[t] * width, width)
+                place = pl.ds(pl.multiple_of(rank_ref[t] * width, width), width)
+                half_ref[:, place] += jnp.dot(
+                    panel_ref[:, pl.ds(lam, width)],
+                    integrals_ref[0, p, 0, k],
+                    preferred_element_type=jnp.float32,
+                )
+
+    total = half_ref.shape[1]
+    step = min(2 * width, total)
+    for n in range(1, -(-total // step) + 1):
+        depth = min(n * step, total)
+
+        @pl.when(pairs_ref[0] == n)
+        def _():
+            out_ref[0] = jnp.dot(
+                half_ref[:, :depth].astype(jnp.bfloat16),
+                vir_ref[:depth, :],
+                preferred_element_type=jnp.float32,
+            ).astype(out_ref.dtype)
+
+
+def transform(lam, rank, used, pairs, integrals, panel, vir):
+    n_occ, n_pair, rows, tile_slots, width, _ = integrals.shape
+    columns, total = panel.shape
+    virtuals = vir.shape[1]
+    return pl.pallas_call(
+        transform_kernel,
+        out_shape=jax.ShapeDtypeStruct((n_occ * rows, columns, virtuals), jnp.bfloat16),
+        grid_spec=pltpu.PrefetchScalarGridSpec(
+            num_scalar_prefetch=4,
+            grid=(n_occ * rows,),
+            in_specs=[
+                pl.BlockSpec(
+                    (1, n_pair, 1, tile_slots, width, width),
+                    lambda r, *_: (r // rows, 0, r % rows, 0, 0, 0),
+                ),
+                pl.BlockSpec((columns, total), lambda r, *_: (0, 0)),
+                pl.BlockSpec((total, virtuals), lambda r, *_: (0, 0)),
+            ],
+            out_specs=pl.BlockSpec((1, columns, virtuals), lambda r, *_: (r, 0, 0)),
+            scratch_shapes=[pltpu.VMEM((columns, total), jnp.float32)],
+        ),
+        compiler_params=pltpu.CompilerParams(vmem_limit_bytes=48 * 2**20),
+    )(lam, rank, used, pairs, integrals, panel, vir)
+
+
+def own_panel(occ_coef, mesh_shape):
+    n_pair, n_occ = mesh_shape["pair"], mesh_shape["occ"]
+    parts = n_pair // n_occ
+    width = occ_coef.shape[1] // parts
+    part = lax.rem(lax.axis_index("pair"), parts)
+    sent = lax.dynamic_slice_in_dim(occ_coef, part * width, width, axis=1)
+    moves = [
+        (a * n_occ + b, (b * parts + a % parts) * n_occ + a // parts)
+        for a in range(n_pair)
+        for b in range(n_occ)
+    ]
+    return lax.ppermute(sent, ("pair", "occ"), moves)
+
+
+def send_integrals(
+    mesh_shape,
+    quarter_integrals,
+    occ_coef,
+    vir_coef,
+    screened_block_mask,
+    tile_holder_pair,
+    shell_size,
+):
+    n_pair, n_occ = mesh_shape["pair"], mesh_shape["occ"]
+    block_count = screened_block_mask.shape[0]
+    rows, tile_slots, slot_width, _ = quarter_integrals.shape
+    gathered = lax.all_gather(quarter_integrals, ("occ", "pair"), axis=0, tiled=False)
+    gathered = gathered.reshape((n_occ, n_pair) + quarter_integrals.shape)
+    panel = trim_rows(own_panel(occ_coef, mesh_shape), shell_size, slot_width).T
+    used, lam, sig = slot_lookup_table(
+        screened_block_mask, tile_holder_pair, n_pair * tile_slots, tile_slots
+    )
+    blocks = jnp.arange(block_count, dtype=jnp.int32)
+    present = jnp.any((sig[:, None] == blocks[None, :]) & (used[:, None] > 0), axis=0)
+    before = present[None, :] & (blocks[None, :] < blocks[:, None])
+    rank_of = jnp.sum(before.astype(jnp.int32), axis=1)
+    rank = jnp.sum((sig[:, None] == blocks[None, :]) * rank_of[None, :], axis=1)
+    held = (rank_of[None, :] == blocks[:, None]) & present[None, :]
+    block_at = jnp.sum(held * blocks[None, :], axis=1)
+    pairs = (jnp.sum(present.astype(jnp.int32)) + 1) // 2
+    inside = jnp.arange(slot_width, dtype=jnp.int32)[None, :] < shell_size[block_at][:, None]
+    vir = vir_coef.reshape(block_count, slot_width, -1)[block_at]
+    vir = jnp.where(inside[:, :, None], vir, jnp.zeros((), vir.dtype)).reshape(vir_coef.shape)
+    return transform(lam, rank, used, pairs.reshape(1), gathered, panel, vir)
+
+
+def pick_plan(mesh_shape):
+    n_pair, n_occ = mesh_shape["pair"], mesh_shape["occ"]
+
+    def per_device(quarter_integrals, occ_coef, vir_coef, *tables):
+        rows, tile_slots, width, _ = quarter_integrals.shape
+        columns = occ_coef.shape[1] * n_occ // n_pair
+        integrals = n_occ * n_pair * quarter_integrals.size
+        transformed = rows * columns * (
+            n_pair * tile_slots * width + n_occ * occ_coef.shape[0]
+        )
+        if n_pair % n_occ == 0 and integrals < transformed:
+            plan = functools.partial(send_integrals, mesh_shape)
+        else:
+            plan = send_tiles
+        return plan(quarter_integrals, occ_coef, vir_coef, *tables)
+
+    return per_device
+
+
 def solution(mesh):
     placed = (
         P(("frag", "occ"), "pair", None, None),
@@ -83,5 +210,5 @@
         P("frag"),
     )
     return jax.shard_map(
-        per_device, mesh=mesh, in_specs=placed, out_specs=P("frag", "pair", "occ"), check_vma=False
-    )
+        pick_plan(dict(mesh.shape)), mesh=mesh, in_specs=placed, out_specs=P("frag", "pair", "occ"), check_vma=False
+    )

time: 297 us -> 135 us (0.45)
  the two profiles are of different devices: /device:TPU:29 before, /device:TPU:0 now
where the time goes in v1:
time: 135 us
  waiting for transfers between devices  59.9 us (44%)
  Pallas kernels  35 us (26%)
  between operations  14.1 us (10%)
  local copies, waits for them, and re-layouts  9.21 us (7%)
  starting transfers between devices  8.88 us (7%)
  other arithmetic  8.11 us (6%)
    all_gather x1, waiting for transfers between devices, send_integrals(): lax.all_gather(quarter_integrals, ('occ', 'pair'), axis=0, tiled=False)  59.2 us
    pallas_call x1, Pallas kernels, transform(): pl.pallas_call(transform_kernel, out_shape=jax.ShapeDtypeStruct((n_occ *...  35 us
    ppermute x1, starting transfers between devices, own_panel(): return lax.ppermute(sent, ('pair', 'occ'), moves)  8.87 us
    unnamed x9, local copies, waits for them, and re-layouts  5.32 us
    select_n x1, other arithmetic, send_integrals(): jnp.where(inside[:, :, None], vir, jnp.zeros((), vir.dtype))  3.53 us
  transfers between devices with their start and end apart: 2, of which 1 were waited for; matrix products, arithmetic and copies ran while one was open for 11% of the time, Pallas kernels for 0%

profile of v1, /device:TPU:0, one launch (start us, length us, event | category | flops | bytes accessed | tf_op | source)
XLA Modules:
  0.0 135.3 jit_solution(3154291479982127482)
XLA Ops:
  6.5 0.0 copy-start
  6.5 0.0 copy-start.3
  6.5 0.0 all-gather.3.cloned.1.call-start
  6.5 0.7 all-gather.3.cloned.1.call-update
  7.3 2.4 %copy.10 = bf16[1280,384]{0,1:T(8,128)(2,1)} copy(bf16[1280,384]{1,0:T(8,128)(2,1)} %param.7) | data formatting | bytes 1966080 | tf_op args[1]
  9.6 8.9 %collective-permute-start = (bf16[1280,384]{0,1:T(8,128)(2,1)}, bf16[1280,384]{0,1:T(8,128)(2,1)}, u32[]{:S(2)}, u32[]{:S(2)}) collective-permute-start(bf16[1280,384]{0,1:T(8,128)(2,1)} %copy.10), channel_id=1, source_target_pairs={{0,0},{1,4},{2,8},{3,12},{4,1},{5,5},{6,9},{7,13},{8,2},{9,6},{10,... | collective-permute-start | bytes 2949128 | tf_op jit(solution)/shard_map/ppermute | solution.py:149
  18.5 0.8 reshape.108
  19.3 0.7 broadcast_compare_fusion
  20.0 0.1 eq.38
  20.1 0.2 convert_reduce_fusion
  20.3 0.2 convert_reduce_fusion.2
  20.5 0.1 fusion.4
  20.5 0.6 convert_reduce_fusion.3
  21.9 0.1 convert_reduce_fusion.1
  22.0 0.1 select_reduce_fusion
  22.1 0.0 copy-done.3
  22.1 0.7 gather_fusion
  22.8 0.0 copy-done
  22.8 2.4 %gather_fusion.1 = bf16[10,128,1024]{2,1,0:T(8,128)(2,1)} fusion(bf16[10,128,1024]{2,1,0:T(8,128)(2,1)S(1)} %bitcast.15, s32[1024]{0:T(1024)S(1)} %pad_clamp_fusion), kind=kCustom, calls=%fused_computation.1 | custom fusion | bytes 5242920 | tf_op jit(solution)/shard_map/gather | solution.py:179
  25.2 0.1 fusion.6
  25.2 0.2 select_reduce_fusion.1.rank_ref
  25.4 0.1 fusion.7
  25.5 3.5 %bitcast_select_fusion.vir_ref = bf16[1280,1024]{1,0:T(8,128)(2,1)} fusion(bf16[10,128,1024]{2,1,0:T(8,128)(2,1)} %gather_fusion.1, pred[1280]{0:T(1024)(128)(4,1)S(1)} %fusion.7), kind=kLoop, calls=%fused_computation.2 | loop fusion | flops 1310720 | bytes 5244160 | tf_op jit(solution)/shard_map/jit(_where)/select_n | solution.py:180
  29.0 0.0 collective-permute-done
  29.0 2.2 %select_bitcast_fusion.panel_ref = bf16[384,1280]{1,0:T(8,128)(2,1)} fusion(bf16[1280,384]{0,1:T(8,128)(2,1)} %collective-permute-done, pred[1280]{0:T(1024)(128)(4,1)S(1)} %fusion.6), kind=kLoop, calls=%fused_computation.3 | loop fusion | flops 491520 | bytes 1967360 | tf_op jit(solution)/shard_map/transpose | solution.py:166
  31.2 59.2 %all-gather.3.cloned.1.call-done = bf16[48,3,128,128]{3,2,1,0:T(8,128)(2,1)} async-done(((bf16[3,3,128,128]{3,2,1,0:T(8,128)(2,1)}), bf16[48,3,128,128]{3,2,1,0:T(8,128)(2,1)}) %all-gather.3.cloned.1.call-update) | async-done | bytes 4718608 | tf_op jit(solution)/shard_map/all_gather | solution.py:164
  90.4 0.0 copy-start.1
  90.4 1.7 %copy-done.1 = bf16[1280,1024]{1,0:T(8,128)(2,1)S(1)} copy-done((bf16[1280,1024]{1,0:T(8,128)(2,1)S(1)}, bf16[1280,1024]{1,0:T(8,128)(2,1)}, u32[]{:S(2)}) %copy-start.1) | copy-done | bytes 2621464
  92.2 0.0 copy-start.2
  92.2 1.2 copy-done.2
  93.4 35.0 %shard_map.64 = bf16[12,384,1024]{2,1,0:T(8,128)(2,1)} custom-call(s32[12]{0:T(128)S(1)} %get-tuple-element.7.lam_ref, s32[12]{0:T(128)S(1)} %select_reduce_fusion.1.rank_ref, s32[12]{0:T(128)S(1)} %get-tuple-element.5.used_ref, s32[1]{0:T(128)} %bitcast.pairs_ref, bf16[4,4,3,3,128,128]{5,4,3,2,1,0:T(8,128)(2,1)} %bitcast.16, ...), custom_call_target="tpu_custom_call" | custom-call | tf_op jit(solution)/shard_map/pallas_call | solution.py:117
  (5 shorter events, 0.0 us)
Async XLA Ops:
  6.5 16.2 %copy-start = (bf16[1280,1024]{1,0:T(8,128)(2,1)S(1)}, bf16[1280,1024]{1,0:T(8,128)(2,1)}, u32[]{:S(2)}) copy-start(bf16[1280,1024]{1,0:T(8,128)(2,1)} %param.8) | copy-start | bytes 7864324
  6.5 15.6 %copy-start.3 = (s32[10]{0:T(128)S(1)}, s32[10]{0:T(128)}, u32[]{:S(2)}) copy-start(s32[10]{0:T(128)} %param.11) | copy-start | bytes 124
  6.5 83.9 %all-gather.3.cloned.1.call-start = ((), (), s32[]{:S(2)}) async-start(), calls=%async_computation | async-start | bytes 5013504 | tf_op jit(solution)/shard_map/all_gather | solution.py:164
  9.6 19.4 %collective-permute-start = (bf16[1280,384]{0,1:T(8,128)(2,1)}, bf16[1280,384]{0,1:T(8,128)(2,1)}, u32[]{:S(2)}, u32[]{:S(2)}) collective-permute-start(bf16[1280,384]{0,1:T(8,128)(2,1)} %copy.10), channel_id=1, source_target_pairs={{0,0},{1,4},{2,8},{3,12},{4,1},{5,5},{6,9},{7,13},{8,2},{9,6},{10,... | collective-permute-start | bytes 2949128 | tf_op jit(solution)/shard_map/ppermute | solution.py:149
  90.4 1.7 %copy-start.1 = (bf16[1280,1024]{1,0:T(8,128)(2,1)S(1)}, bf16[1280,1024]{1,0:T(8,128)(2,1)}, u32[]{:S(2)}) copy-start(bf16[1280,1024]{1,0:T(8,128)(2,1)} %bitcast_select_fusion.vir_ref) | copy-start | bytes 7864324
  92.2 1.2 copy-start.2
Sparse Core Ops, SparseCore 0:
  9.7 80.7 all-gather.2

commit v2 on v1

--- a/solution.py
+++ b/solution.py
@@ -77,10 +77,189 @@
     ).astype(jnp.bfloat16)
 
 
+MESH = pl.DeviceIdType.MESH
+
+
+def gather_kernel(
+    n_pair, n_occ, integrals_ref, shard_ref, all_ref, panel_ref, local, z_send, z_recv,
+    x_send, x_recv, core_send, core_recv, panel_send, panel_recv,
+):
+    cores = 2
+    n_x = n_occ // cores
+    z, occ = lax.axis_index("pair"), lax.axis_index("occ")
+    x, core = occ // cores, lax.rem(occ, cores)
+    sibling = x * cores + 1 - core
+    holder = z // (n_pair // n_occ)
+    holder_x, holder_core = holder // cores, lax.rem(holder, cores)
+    z_peers = [lax.rem(z + d, n_pair) for d in range(1, n_pair)]
+    x_peers = [lax.rem(x + d, n_x) for d in range(1, n_x)]
+
+    barrier = pltpu.get_barrier_semaphore()
+    for peer in z_peers:
+        pl.semaphore_signal(barrier, inc=1, device_id={"pair": peer}, device_id_type=MESH)
+    for peer in x_peers:
+        pl.semaphore_signal(
+            barrier, inc=1, device_id={"occ": peer * cores + core}, device_id_type=MESH
+        )
+    pl.semaphore_signal(barrier, inc=1, device_id={"occ": sibling}, device_id_type=MESH)
+    pl.semaphore_wait(barrier, n_pair + n_x - 1)
+
+    def along_z(d):
+        return pltpu.make_async_remote_copy(
+            src_ref=integrals_ref,
+            dst_ref=all_ref.at[occ, z],
+            send_sem=z_send.at[d],
+            recv_sem=z_recv.at[d],
+            device_id={"pair": lax.rem(z + d, n_pair)},
+            device_id_type=MESH,
+        )
+
+    def block(x_of, d):
+        return all_ref.at[x_of * cores + core, lax.rem(z + n_pair - d, n_pair)]
+
+    def across_x(e, d):
+        source = integrals_ref if d == 0 else block(x, d)
+        return pltpu.make_async_remote_copy(
+            src_ref=source,
+            dst_ref=block(x, d),
+            send_sem=x_send.at[e, d],
+            recv_sem=x_recv.at[e, d],
+            device_id={"occ": lax.rem(x + e, n_x) * cores + core},
+            device_id_type=MESH,
+        )
+
+    def across_cores(e, d):
+        x_of = lax.rem(x + n_x - e, n_x)
+        source = integrals_ref if d == 0 and e == 0 else block(x_of, d)
+        return pltpu.make_async_remote_copy(
+            src_ref=source,
+            dst_ref=block(x_of, d),
+            send_sem=core_send.at[e, d],
+            recv_sem=core_recv.at[e, d],
+            device_id={"occ": sibling},
+            device_id_type=MESH,
+        )
+
+    def panel_to(place, source, target):
+        return pltpu.make_async_remote_copy(
+            src_ref=source,
+            dst_ref=panel_ref,
+            send_sem=panel_send.at[place],
+            recv_sem=panel_recv,
+            device_id={"occ": target},
+            device_id_type=MESH,
+        )
+
+    holds = occ == holder
+    passes_on = jnp.logical_and(core == holder_core, x != holder_x)
+
+    for d in range(1, n_pair):
+        along_z(d).start()
+    for e in range(1, n_x):
+        across_x(e, 0).start()
+    own = pltpu.make_async_copy(integrals_ref, all_ref.at[occ, z], local.at[0])
+    own.start()
+    own_panel = pltpu.make_async_copy(shard_ref, panel_ref, local.at[1])
+
+    @pl.when(holds)
+    def _():
+        for e in range(1, n_x):
+            panel_to(e, shard_ref, lax.rem(x + e, n_x) * cores + core).start()
+        panel_to(0, shard_ref, sibling).start()
+        own_panel.start()
+
+    across_cores(0, 0).start()
+    for d in range(1, n_pair):
+        along_z(d).wait_recv()
+        for e in range(1, n_x):
+            across_x(e, d).start()
+        across_cores(0, d).start()
+
+    @pl.when(passes_on)
+    def _():
+        panel_to(0, panel_ref, sibling).wait_recv()
+        panel_to(0, panel_ref, sibling).start()
+
+    for d in range(n_pair):
+        for e in range(1, n_x):
+            across_x(e, d).wait_recv()
+            across_cores(e, d).start()
+
+    @pl.when(core != holder_core)
+    def _():
+        panel_to(0, panel_ref, sibling).wait_recv()
+
+    for e in range(n_x):
+        for d in range(n_pair):
+            across_cores(e, d).wait()
+    for e in range(1, n_x):
+        for d in range(n_pair):
+            across_x(e, d).wait_send()
+    for d in range(1, n_pair):
+        along_z(d).wait_send()
+    own.wait()
+
+    @pl.when(holds)
+    def _():
+        for e in range(1, n_x):
+            panel_to(e, shard_ref, sibling).wait_send()
+        panel_to(0, shard_ref, sibling).wait_send()
+        own_panel.wait()
+
+    @pl.when(passes_on)
+    def _():
+        panel_to(0, panel_ref, sibling).wait_send()
+
+
+def gather(mesh_shape, integrals, shard):
+    n_pair, n_occ = mesh_shape["pair"], mesh_shape["occ"]
+    n_x = n_occ // 2
+    return pl.pallas_call(
+        functools.partial(gather_kernel, n_pair, n_occ),
+        out_shape=(
+            jax.ShapeDtypeStruct((n_occ, n_pair) + integrals.shape, integrals.dtype),
+            jax.ShapeDtypeStruct(shard.shape, shard.dtype),
+        ),
+        in_specs=[pl.BlockSpec(memory_space=pl.ANY)] * 2,
+        out_specs=(pl.BlockSpec(memory_space=pl.ANY),) * 2,
+        scratch_shapes=[
+            pltpu.SemaphoreType.DMA((2,)),
+            pltpu.SemaphoreType.DMA((n_pair,)),
+            pltpu.SemaphoreType.DMA((n_pair,)),
+            pltpu.SemaphoreType.DMA((n_x, n_pair)),
+            pltpu.SemaphoreType.DMA((n_x, n_pair)),
+            pltpu.SemaphoreType.DMA((n_x, n_pair)),
+            pltpu.SemaphoreType.DMA((n_x, n_pair)),
+            pltpu.SemaphoreType.DMA((n_x,)),
+            pltpu.SemaphoreType.DMA,
+        ],
+        compiler_params=pltpu.CompilerParams(collective_id=0, has_side_effects=True),
+    )(integrals, shard)
+
+
 def transform_kernel(
-    lam_ref, rank_ref, used_ref, pairs_ref, integrals_ref, panel_ref, vir_ref, out_ref, half_ref
+    lam_ref, rank_ref, used_ref, at_ref, size_ref, count_ref,
+    integrals_ref, panel_ref, vir_ref, out_ref, half_ref, kept_ref,
 ):
-    n_pair, _, tile_slots, width, _ = integrals_ref.shape[1:]
+    n_pair, rows, tile_slots, width, _ = integrals_ref.shape[1:]
+    columns, total = panel_ref.shape
+    step = min(2 * width, total)
+
+    @pl.when(pl.program_id(0) == 0)
+    def _():
+        kept_ref[...] = jnp.zeros_like(kept_ref)
+        for i in range(total // width):
+
+            @pl.when(i < count_ref[0])
+            def _():
+                block = at_ref[i]
+                shape = (width, vir_ref.shape[1])
+                inside = lax.broadcasted_iota(jnp.int32, shape, 0) < size_ref[block]
+                found = vir_ref[pl.ds(pl.multiple_of(block * width, width), width), :]
+                kept_ref[i * width : (i + 1) * width, :] = jnp.where(
+                    inside, found.astype(jnp.float32), 0.0
+                ).astype(kept_ref.dtype)
+
     half_ref[...] = jnp.zeros_like(half_ref)
     for p in range(n_pair):
         for k in range(tile_slots):
@@ -90,27 +269,27 @@
             def _():
                 lam = pl.multiple_of(lam_ref[t] * width, width)
                 place = pl.ds(pl.multiple_of(rank_ref[t] * width, width), width)
-                half_ref[:, place] += jnp.dot(
-                    panel_ref[:, pl.ds(lam, width)],
-                    integrals_ref[0, p, 0, k],
-                    preferred_element_type=jnp.float32,
+                tiles = jnp.concatenate([integrals_ref[0, p, r, k] for r in range(rows)], axis=1)
+                part = jnp.dot(
+                    panel_ref[:, pl.ds(lam, width)], tiles, preferred_element_type=jnp.float32
                 )
-
-    total = half_ref.shape[1]
-    step = min(2 * width, total)
+                for r in range(rows):
+                    half_ref[r, :, place] += part[:, r * width : (r + 1) * width]
+
     for n in range(1, -(-total // step) + 1):
         depth = min(n * step, total)
 
-        @pl.when(pairs_ref[0] == n)
+        @pl.when((count_ref[0] * width + step - 1) // step == n)
         def _():
-            out_ref[0] = jnp.dot(
-                half_ref[:, :depth].astype(jnp.bfloat16),
-                vir_ref[:depth, :],
-                preferred_element_type=jnp.float32,
-            ).astype(out_ref.dtype)
-
-
-def transform(lam, rank, used, pairs, integrals, panel, vir):
+            for r in range(rows):
+                out_ref[r] = jnp.dot(
+                    half_ref[r, :, :depth].astype(jnp.bfloat16),
+                    kept_ref[:depth, :],
+                    preferred_element_type=jnp.float32,
+                ).astype(out_ref.dtype)
+
+
+def transform(lam, rank, used, block_at, shell_size, count, integrals, panel, vir):
     n_occ, n_pair, rows, tile_slots, width, _ = integrals.shape
     columns, total = panel.shape
     virtuals = vir.shape[1]
@@ -118,35 +297,24 @@
         transform_kernel,
         out_shape=jax.ShapeDtypeStruct((n_occ * rows, columns, virtuals), jnp.bfloat16),
         grid_spec=pltpu.PrefetchScalarGridSpec(
-            num_scalar_prefetch=4,
-            grid=(n_occ * rows,),
+            num_scalar_prefetch=6,
+            grid=(n_occ,),
             in_specs=[
                 pl.BlockSpec(
-                    (1, n_pair, 1, tile_slots, width, width),
-                    lambda r, *_: (r // rows, 0, r % rows, 0, 0, 0),
+                    (1, n_pair, rows, tile_slots, width, width),
+                    lambda o, *_: (o, 0, 0, 0, 0, 0),
                 ),
-                pl.BlockSpec((columns, total), lambda r, *_: (0, 0)),
-                pl.BlockSpec((total, virtuals), lambda r, *_: (0, 0)),
+                pl.BlockSpec((columns, total), lambda o, *_: (0, 0)),
+                pl.BlockSpec((total, virtuals), lambda o, *_: (0, 0)),
             ],
-            out_specs=pl.BlockSpec((1, columns, virtuals), lambda r, *_: (r, 0, 0)),
-            scratch_shapes=[pltpu.VMEM((columns, total), jnp.float32)],
+            out_specs=pl.BlockSpec((rows, columns, virtuals), lambda o, *_: (o, 0, 0)),
+            scratch_shapes=[
+                pltpu.VMEM((rows, columns, total), jnp.float32),
+                pltpu.VMEM((total, virtuals), jnp.bfloat16),
+            ],
         ),
-        compiler_params=pltpu.CompilerParams(vmem_limit_bytes=48 * 2**20),
-    )(lam, rank, used, pairs, integrals, panel, vir)
-
-
-def own_panel(occ_coef, mesh_shape):
-    n_pair, n_occ = mesh_shape["pair"], mesh_shape["occ"]
-    parts = n_pair // n_occ
-    width = occ_coef.shape[1] // parts
-    part = lax.rem(lax.axis_index("pair"), parts)
-    sent = lax.dynamic_slice_in_dim(occ_coef, part * width, width, axis=1)
-    moves = [
-        (a * n_occ + b, (b * parts + a % parts) * n_occ + a // parts)
-        for a in range(n_pair)
-        for b in range(n_occ)
-    ]
-    return lax.ppermute(sent, ("pair", "occ"), moves)
+        compiler_params=pltpu.CompilerParams(vmem_limit_bytes=56 * 2**20),
+    )(lam, rank, used, block_at, shell_size, count, integrals, panel, vir)
 
 
 def send_integrals(
@@ -161,9 +329,14 @@
     n_pair, n_occ = mesh_shape["pair"], mesh_shape["occ"]
     block_count = screened_block_mask.shape[0]
     rows, tile_slots, slot_width, _ = quarter_integrals.shape
-    gathered = lax.all_gather(quarter_integrals, ("occ", "pair"), axis=0, tiled=False)
-    gathered = gathered.reshape((n_occ, n_pair) + quarter_integrals.shape)
-    panel = trim_rows(own_panel(occ_coef, mesh_shape), shell_size, slot_width).T
+    parts = n_pair // n_occ
+    shard = occ_coef
+    if parts > 1:
+        wide = occ_coef.shape[1] // parts
+        part = lax.rem(lax.axis_index("pair"), parts)
+        shard = lax.dynamic_slice_in_dim(occ_coef, part * wide, wide, axis=1)
+    gathered, panel = gather(mesh_shape, quarter_integrals, shard)
+    panel = trim_rows(panel, shell_size, slot_width).T
     used, lam, sig = slot_lookup_table(
         screened_block_mask, tile_holder_pair, n_pair * tile_slots, tile_slots
     )
@@ -174,11 +347,10 @@
     rank = jnp.sum((sig[:, None] == blocks[None, :]) * rank_of[None, :], axis=1)
     held = (rank_of[None, :] == blocks[:, None]) & present[None, :]
     block_at = jnp.sum(held * blocks[None, :], axis=1)
-    pairs = (jnp.sum(present.astype(jnp.int32)) + 1) // 2
-    inside = jnp.arange(slot_width, dtype=jnp.int32)[None, :] < shell_size[block_at][:, None]
-    vir = vir_coef.reshape(block_count, slot_width, -1)[block_at]
-    vir = jnp.where(inside[:, :, None], vir, jnp.zeros((), vir.dtype)).reshape(vir_coef.shape)
-    return transform(lam, rank, used, pairs.reshape(1), gathered, panel, vir)
+    count = jnp.sum(present.astype(jnp.int32)).reshape(1)
+    return transform(
+        lam, rank, used, block_at, shell_size, count, gathered, panel, vir_coef
+    )
 
 
 def pick_plan(mesh_shape):
@@ -191,7 +363,7 @@
         transformed = rows * columns * (
             n_pair * tile_slots * width + n_occ * occ_coef.shape[0]
         )
-        if n_pair % n_occ == 0 and integrals < transformed:
+        if n_occ % 2 == 0 and n_pair % n_occ == 0 and integrals < transformed:
             plan = functools.partial(send_integrals, mesh_shape)
         else:
             plan = send_tiles

time: 135 us -> 76.2 us (0.56)
  the two profiles are of different devices: /device:TPU:0 before, /device:TPU:29 now
where the time goes in v2:
time: 76.2 us; the launch traced here: 76.8 us
  Pallas kernels  68.7 us (90%)
  other arithmetic  5.67 us (7%)
  local copies, waits for them, and re-layouts  2.42 us (3%)
    pallas_call x1, Pallas kernels, gather(): pl.pallas_call(functools.partial(gather_kernel, n_pair, n_occ), out_shape...  45.7 us
    pallas_call x1, Pallas kernels, transform(): pl.pallas_call(transform_kernel, out_shape=jax.ShapeDtypeStruct((n_occ *...  23 us
    pallas_call x1, local copies, waits for them, and re-layouts, gather(): pl.pallas_call(functools.partial(gather_kernel, n_pair, n_occ), out_shape...  1.55 us

profile of v2, /device:TPU:29, one launch (start us, length us, event | category | flops | bytes accessed | tf_op | source)
XLA Modules:
  0.0 76.8 jit_solution(12112547179919840770)
XLA Ops:
  0.0 0.8 %reshape.66 = s32[100]{0:T(128)S(1)} reshape(s32[10,10]{1,0:T(8,128)} %param.10) | data formatting | bytes 800 | tf_op jit(solution)/shard_map/reshape | solution.py:14
  0.8 0.7 broadcast_compare_fusion
  1.5 0.1 eq.38
  1.6 0.2 convert_reduce_fusion
  1.8 0.6 convert_reduce_fusion.2
  2.4 0.0 copy-start
  2.4 0.1 fusion.4
  2.5 0.7 convert_reduce_fusion.3
  3.2 0.1 convert_reduce_fusion.1
  3.4 0.7 select_reduce_fusion.at_ref
  4.0 0.8 select_reduce_fusion.1.rank_ref
  4.8 0.7 fusion.7
  5.5 45.7 %shard_map.64 = (bf16[4,4,3,3,128,128]{5,4,3,2,1,0:T(8,128)(2,1)}, bf16[1280,384]{1,0:T(8,128)(2,1)}) custom-call(bf16[3,3,128,128]{3,2,1,0:T(8,128)(2,1)} %integrals_ref.1, bf16[1280,384]{1,0:T(8,128)(2,1)} %shard_ref.1), custom_call_target="tpu_custom_call" | custom-call | tf_op jit(solution)/shard_map/pallas_call | solution.py:217
  51.2 1.6 %copy.8 = bf16[1280,384]{0,1:T(8,128)(2,1)S(1)} copy(bf16[1280,384]{1,0:T(8,128)(2,1)} %get-tuple-element.8) | data formatting | bytes 1966080 | tf_op jit(solution)/shard_map/pallas_call | solution.py:217
  52.8 1.1 %select_bitcast_fusion.panel_ref = bf16[384,1280]{1,0:T(8,128)(2,1)} fusion(bf16[1280,384]{0,1:T(8,128)(2,1)S(1)} %copy.8, pred[1280]{0:T(1024)(128)(4,1)S(1)} %fusion.7), kind=kLoop, calls=%fused_computation | loop fusion | flops 491520 | bytes 1967360 | tf_op jit(solution)/shard_map/transpose | solution.py:339
  53.8 0.0 copy-done
  53.8 23.0 %shard_map.65 = bf16[12,384,1024]{2,1,0:T(8,128)(2,1)} custom-call(s32[12]{0:T(128)} %get-tuple-element.11.lam_ref, s32[12]{0:T(128)} %select_reduce_fusion.1.rank_ref, s32[12]{0:T(128)} %copy-done, s32[10]{0:T(128)} %select_reduce_fusion.at_ref, s32[10]{0:T(128)} %size_ref.1, s32[1]{0:T(128)} %bitcast.count_ref, ...), custom_call_target="tpu_custom_call" | custom-call | tf_op jit(solution)/shard_map/pallas_call | solution.py:296
  (3 shorter events, 0.0 us)
Async XLA Ops:
  2.4 51.4 %copy-start = (s32[12]{0:T(128)}, s32[12]{0:T(128)S(1)}, u32[]{:S(2)}) copy-start(s32[12]{0:T(128)S(1)} %get-tuple-element.9.used_ref) | copy-start | bytes 148

commit v3 on v2

--- a/solution.py
+++ b/solution.py
@@ -81,8 +81,9 @@
 
 
 def gather_kernel(
-    n_pair, n_occ, integrals_ref, shard_ref, all_ref, panel_ref, local, z_send, z_recv,
-    x_send, x_recv, core_send, core_recv, panel_send, panel_recv,
+    n_pair, n_occ, size_ref, mask_ref, owner_ref, integrals_ref, shard_ref,
+    all_ref, turned_ref, slots_ref, panel_ref, local, z_send, z_recv, x_send, x_recv,
+    core_send, core_recv, panel_send, panel_recv,
 ):
     cores = 2
     n_x = n_occ // cores
@@ -155,8 +156,6 @@
 
     for d in range(1, n_pair):
         along_z(d).start()
-    for e in range(1, n_x):
-        across_x(e, 0).start()
     own = pltpu.make_async_copy(integrals_ref, all_ref.at[occ, z], local.at[0])
     own.start()
     own_panel = pltpu.make_async_copy(shard_ref, panel_ref, local.at[1])
@@ -168,7 +167,10 @@
         panel_to(0, shard_ref, sibling).start()
         own_panel.start()
 
+    for e in range(1, n_x):
+        across_x(e, 0).start()
     across_cores(0, 0).start()
+    write_slots(n_pair, mask_ref, owner_ref, slots_ref)
     for d in range(1, n_pair):
         along_z(d).wait_recv()
         for e in range(1, n_x):
@@ -180,14 +182,19 @@
         panel_to(0, panel_ref, sibling).wait_recv()
         panel_to(0, panel_ref, sibling).start()
 
+    @pl.when(core != holder_core)
+    def _():
+        panel_to(0, panel_ref, sibling).wait_recv()
+
+    @pl.when(holds)
+    def _():
+        own_panel.wait()
+
+    turn_panel(size_ref, panel_ref, turned_ref)
     for d in range(n_pair):
         for e in range(1, n_x):
             across_x(e, d).wait_recv()
             across_cores(e, d).start()
-
-    @pl.when(core != holder_core)
-    def _():
-        panel_to(0, panel_ref, sibling).wait_recv()
 
     for e in range(n_x):
         for d in range(n_pair):
@@ -204,25 +211,37 @@
         for e in range(1, n_x):
             panel_to(e, shard_ref, sibling).wait_send()
         panel_to(0, shard_ref, sibling).wait_send()
-        own_panel.wait()
 
     @pl.when(passes_on)
     def _():
         panel_to(0, panel_ref, sibling).wait_send()
 
 
-def gather(mesh_shape, integrals, shard):
+def gather(mesh_shape, shell_size, mask, owner, integrals, shard):
     n_pair, n_occ = mesh_shape["pair"], mesh_shape["occ"]
     n_x = n_occ // 2
+    slots = n_pair * integrals.shape[1]
     return pl.pallas_call(
         functools.partial(gather_kernel, n_pair, n_occ),
         out_shape=(
             jax.ShapeDtypeStruct((n_occ, n_pair) + integrals.shape, integrals.dtype),
-            jax.ShapeDtypeStruct(shard.shape, shard.dtype),
+            jax.ShapeDtypeStruct(shard.shape[::-1], shard.dtype),
+            jax.ShapeDtypeStruct((3 * slots,), jnp.int32),
         ),
-        in_specs=[pl.BlockSpec(memory_space=pl.ANY)] * 2,
-        out_specs=(pl.BlockSpec(memory_space=pl.ANY),) * 2,
+        in_specs=[
+            pl.BlockSpec(memory_space=pltpu.SMEM),
+            pl.BlockSpec(memory_space=pltpu.VMEM),
+            pl.BlockSpec(memory_space=pltpu.VMEM),
+            pl.BlockSpec(memory_space=pl.ANY),
+            pl.BlockSpec(memory_space=pl.ANY),
+        ],
+        out_specs=(
+            pl.BlockSpec(memory_space=pl.ANY),
+            pl.BlockSpec(memory_space=pltpu.VMEM),
+            pl.BlockSpec(memory_space=pltpu.SMEM),
+        ),
         scratch_shapes=[
+            pltpu.VMEM(shard.shape, shard.dtype),
             pltpu.SemaphoreType.DMA((2,)),
             pltpu.SemaphoreType.DMA((n_pair,)),
             pltpu.SemaphoreType.DMA((n_pair,)),
@@ -233,24 +252,74 @@
             pltpu.SemaphoreType.DMA((n_x,)),
             pltpu.SemaphoreType.DMA,
         ],
-        compiler_params=pltpu.CompilerParams(collective_id=0, has_side_effects=True),
-    )(integrals, shard)
+        compiler_params=pltpu.CompilerParams(
+            collective_id=0, has_side_effects=True, vmem_limit_bytes=24 * 2**20
+        ),
+    )(shell_size, mask, owner, integrals, shard)
+
+
+def write_slots(n_pair, mask_ref, owner_ref, slots_ref):
+    shape = mask_ref.shape
+    tile_slots = slots_ref.shape[0] // (3 * n_pair)
+    row = lax.broadcasted_iota(jnp.int32, shape, 0)
+    column = lax.broadcasted_iota(jnp.int32, shape, 1)
+    before = (row < column).astype(jnp.float32)
+    kept, owner = mask_ref[...] == 1, owner_ref[...]
+    rows_of, columns_of = row.astype(jnp.float32), column.astype(jnp.float32)
+    for p in range(n_pair):
+        owned = (kept & (owner == p)).astype(jnp.float32)
+        in_row = jnp.dot(owned, before, preferred_element_type=jnp.float32)
+        sums = jnp.broadcast_to(jnp.sum(owned, axis=1, keepdims=True), shape)
+        above = jnp.zeros(shape, jnp.float32)
+        for i in range(shape[0]):
+            above += jnp.where(row > i, sums[i : i + 1, :], 0.0)
+        rank = in_row + above
+        for k in range(tile_slots):
+            chosen = jnp.where(rank == float(k), owned, 0.0)
+            t = p * tile_slots + k
+            slots_ref[3 * t] = jnp.sum(chosen).astype(jnp.int32)
+            slots_ref[3 * t + 1] = jnp.sum(chosen * rows_of).astype(jnp.int32)
+            slots_ref[3 * t + 2] = jnp.sum(chosen * columns_of).astype(jnp.int32)
+
+
+def turn_panel(size_ref, panel_ref, turned_ref):
+    total, columns = panel_ref.shape
+    blocks = size_ref.shape[0]
+    width = total // blocks
+    place = lax.broadcasted_iota(jnp.int32, (width, columns), 0)
+    for i in range(blocks):
+        found = panel_ref[i * width : (i + 1) * width, :].astype(jnp.float32)
+        used = jnp.where(place < size_ref[i], found, 0.0)
+        turned_ref[:, i * width : (i + 1) * width] = used.T.astype(turned_ref.dtype)
 
 
 def transform_kernel(
-    lam_ref, rank_ref, used_ref, at_ref, size_ref, count_ref,
-    integrals_ref, panel_ref, vir_ref, out_ref, half_ref, kept_ref,
+    slots_ref, size_ref, integrals_ref, panel_ref, vir_ref, out_ref,
+    half_ref, kept_ref, rank_ref, first_ref, at_ref, count_ref,
 ):
     n_pair, rows, tile_slots, width, _ = integrals_ref.shape[1:]
     columns, total = panel_ref.shape
+    blocks = total // width
     step = min(2 * width, total)
 
     @pl.when(pl.program_id(0) == 0)
     def _():
-        kept_ref[...] = jnp.zeros_like(kept_ref)
-        for i in range(total // width):
-
-            @pl.when(i < count_ref[0])
+        count = jnp.int32(0)
+        for t in range(n_pair * tile_slots):
+            sig, rank, first = slots_ref[3 * t + 2], count, jnp.int32(1)
+            for u in range(t):
+                same = (slots_ref[3 * u] > 0) & (slots_ref[3 * u + 2] == sig)
+                rank = jnp.where(same, rank_ref[u], rank)
+                first = jnp.where(same, 0, first)
+            rank_ref[t] = rank
+            first_ref[t] = first
+            at_ref[count] = sig
+            count += first * slots_ref[3 * t]
+        count_ref[0] = count
+        half_ref[...] = jnp.zeros_like(half_ref)
+        for i in range(blocks):
+
+            @pl.when(i < count)
             def _():
                 block = at_ref[i]
                 shape = (width, vir_ref.shape[1])
@@ -260,44 +329,65 @@
                     inside, found.astype(jnp.float32), 0.0
                 ).astype(kept_ref.dtype)
 
-    half_ref[...] = jnp.zeros_like(half_ref)
+            @pl.when(i >= count)
+            def _():
+                kept_ref[i * width : (i + 1) * width, :] = jnp.zeros(
+                    (width, vir_ref.shape[1]), kept_ref.dtype
+                )
+
     for p in range(n_pair):
         for k in range(tile_slots):
             t = p * tile_slots + k
 
-            @pl.when(used_ref[t] > 0)
+            @pl.when(slots_ref[3 * t] > 0)
             def _():
-                lam = pl.multiple_of(lam_ref[t] * width, width)
+                lam = pl.multiple_of(slots_ref[3 * t + 1] * width, width)
                 place = pl.ds(pl.multiple_of(rank_ref[t] * width, width), width)
                 tiles = jnp.concatenate([integrals_ref[0, p, r, k] for r in range(rows)], axis=1)
                 part = jnp.dot(
                     panel_ref[:, pl.ds(lam, width)], tiles, preferred_element_type=jnp.float32
                 )
-                for r in range(rows):
-                    half_ref[r, :, place] += part[:, r * width : (r + 1) * width]
+
+                @pl.when(first_ref[t] > 0)
+                def _():
+                    for r in range(rows):
+                        half_ref[r * columns : (r + 1) * columns, place] = part[
+                            :, r * width : (r + 1) * width
+                        ]
+
+                @pl.when(first_ref[t] == 0)
+                def _():
+                    for r in range(rows):
+                        half_ref[r * columns : (r + 1) * columns, place] += part[
+                            :, r * width : (r + 1) * width
+                        ]
 
     for n in range(1, -(-total // step) + 1):
         depth = min(n * step, total)
 
         @pl.when((count_ref[0] * width + step - 1) // step == n)
         def _():
-            for r in range(rows):
-                out_ref[r] = jnp.dot(
-                    half_ref[r, :, :depth].astype(jnp.bfloat16),
+            out_ref[...] = (
+                jnp.dot(
+                    half_ref[:, :depth].astype(jnp.bfloat16),
                     kept_ref[:depth, :],
                     preferred_element_type=jnp.float32,
-                ).astype(out_ref.dtype)
-
-
-def transform(lam, rank, used, block_at, shell_size, count, integrals, panel, vir):
+                )
+                .astype(out_ref.dtype)
+                .reshape(out_ref.shape)
+            )
+
+
+def transform(slots, shell_size, integrals, panel, vir):
     n_occ, n_pair, rows, tile_slots, width, _ = integrals.shape
     columns, total = panel.shape
     virtuals = vir.shape[1]
+    count = n_pair * tile_slots
     return pl.pallas_call(
         transform_kernel,
         out_shape=jax.ShapeDtypeStruct((n_occ * rows, columns, virtuals), jnp.bfloat16),
         grid_spec=pltpu.PrefetchScalarGridSpec(
-            num_scalar_prefetch=6,
+            num_scalar_prefetch=2,
             grid=(n_occ,),
             in_specs=[
                 pl.BlockSpec(
@@ -309,12 +399,16 @@
             ],
             out_specs=pl.BlockSpec((rows, columns, virtuals), lambda o, *_: (o, 0, 0)),
             scratch_shapes=[
-                pltpu.VMEM((rows, columns, total), jnp.float32),
+                pltpu.VMEM((rows * columns, total), jnp.float32),
                 pltpu.VMEM((total, virtuals), jnp.bfloat16),
+                pltpu.SMEM((count,), jnp.int32),
+                pltpu.SMEM((count,), jnp.int32),
+                pltpu.SMEM((total // width + 1,), jnp.int32),
+                pltpu.SMEM((1,), jnp.int32),
             ],
         ),
         compiler_params=pltpu.CompilerParams(vmem_limit_bytes=56 * 2**20),
-    )(lam, rank, used, block_at, shell_size, count, integrals, panel, vir)
+    )(slots, shell_size, integrals, panel, vir)
 
 
 def send_integrals(
@@ -326,31 +420,16 @@
     tile_holder_pair,
     shell_size,
 ):
-    n_pair, n_occ = mesh_shape["pair"], mesh_shape["occ"]
-    block_count = screened_block_mask.shape[0]
-    rows, tile_slots, slot_width, _ = quarter_integrals.shape
-    parts = n_pair // n_occ
+    parts = mesh_shape["pair"] // mesh_shape["occ"]
     shard = occ_coef
     if parts > 1:
         wide = occ_coef.shape[1] // parts
         part = lax.rem(lax.axis_index("pair"), parts)
         shard = lax.dynamic_slice_in_dim(occ_coef, part * wide, wide, axis=1)
-    gathered, panel = gather(mesh_shape, quarter_integrals, shard)
-    panel = trim_rows(panel, shell_size, slot_width).T
-    used, lam, sig = slot_lookup_table(
-        screened_block_mask, tile_holder_pair, n_pair * tile_slots, tile_slots
-    )
-    blocks = jnp.arange(block_count, dtype=jnp.int32)
-    present = jnp.any((sig[:, None] == blocks[None, :]) & (used[:, None] > 0), axis=0)
-    before = present[None, :] & (blocks[None, :] < blocks[:, None])
-    rank_of = jnp.sum(before.astype(jnp.int32), axis=1)
-    rank = jnp.sum((sig[:, None] == blocks[None, :]) * rank_of[None, :], axis=1)
-    held = (rank_of[None, :] == blocks[:, None]) & present[None, :]
-    block_at = jnp.sum(held * blocks[None, :], axis=1)
-    count = jnp.sum(present.astype(jnp.int32)).reshape(1)
-    return transform(
-        lam, rank, used, block_at, shell_size, count, gathered, panel, vir_coef
-    )
+    gathered, panel, slots = gather(
+        mesh_shape, shell_size, screened_block_mask, tile_holder_pair, quarter_integrals, shard
+    )
+    return transform(slots, shell_size, gathered, panel, vir_coef)
 
 
 def pick_plan(mesh_shape):

time: 76.2 us -> 75.9 us (level); the launches traced: 76.8 us -> 75.1 us
  other arithmetic: 5.67 us -> 0 us
  local copies, waits for them, and re-layouts: 2.42 us -> 7.88 us
  Pallas kernels: 68.7 us -> 67.2 us
    unnamed x2 -> x16, local copies, waits for them, and re-layouts: 0.01 us -> 7.88 us
    reduce_sum x6 -> x0, other arithmetic: 3.08 us -> none  [the longest x1 0.76 us: send_integrals(): rank = jnp.sum((sig[:, None] == blocks[None, :]) * rank_of[None, :], axis=1)]
    pallas_call x1, Pallas kernels: 23 us -> 21.3 us  [transform(): pl.pallas_call(transform_kernel, out_shape=jax.ShapeDtypeStruct((n_occ *...]
    pallas_call x1 -> x0, local copies, waits for them, and re-layouts: 1.55 us -> none  [gather(): pl.pallas_call(functools.partial(gather_kernel, n_pair, n_occ), out_shape...]
    transpose x1 -> x0, other arithmetic: 1.05 us -> none  [send_integrals(): panel = trim_rows(panel, shell_size, slot_width).T]
    reshape x1 -> x0, local copies, waits for them, and re-layouts: 0.78 us -> none  [slot_lookup_table(): owners = tile_holder_pair.reshape(-1)]
where the time goes in v3:
time: 75.9 us; the launch traced here: 75.1 us
  Pallas kernels  67.2 us (89%)
  local copies, waits for them, and re-layouts  7.88 us (10%)
    pallas_call x1, Pallas kernels, gather(): pl.pallas_call(functools.partial(gather_kernel, n_pair, n_occ), out_shape...  45.9 us
    pallas_call x1, Pallas kernels, transform(): pl.pallas_call(transform_kernel, out_shape=jax.ShapeDtypeStruct((n_occ *...  21.3 us
    unnamed x16, local copies, waits for them, and re-layouts  7.88 us

profile of v3, /device:TPU:29, one launch (start us, length us, event | category | flops | bytes accessed | tf_op | source)
XLA Modules:
  0.0 75.1 jit_solution(17182580584887107961)
XLA Ops:
  0.0 0.0 copy-start.1
  0.0 1.2 %copy-done.1 = bf16[1280,384]{1,0:T(8,128)(2,1)S(1)} copy-done((bf16[1280,384]{1,0:T(8,128)(2,1)S(1)}, bf16[1280,384]{1,0:T(8,128)(2,1)}, u32[]{:S(2)}) %copy-start.1) | copy-done | bytes 983064
  1.2 0.0 copy-start.3
  1.2 1.0 %copy-done.3 = bf16[3,3,128,128]{3,2,1,0:T(8,128)(2,1)S(1)} copy-done((bf16[3,3,128,128]{3,2,1,0:T(8,128)(2,1)S(1)}, bf16[3,3,128,128]{3,2,1,0:T(8,128)(2,1)}, u32[]{:S(2)}) %copy-start.3) | copy-done | bytes 294936
  2.2 0.0 copy-start.4
  2.2 0.7 copy-done.4
  2.9 0.0 copy-start.5
  2.9 0.7 copy-done.5
  3.6 0.0 copy-start.6
  3.6 0.7 copy-done.6
  4.2 45.9 %shard_map.64 = (bf16[4,4,3,3,128,128]{5,4,3,2,1,0:T(8,128)(2,1)S(1)}, bf16[384,1280]{1,0:T(8,128)(2,1)S(1)}, s32[36]{0:T(128)S(1)}) custom-call(s32[10]{0:T(128)S(1)} %copy-done.6, s32[10,10]{1,0:T(8,128)S(1)} %copy-done.4, s32[10,10]{1,0:T(8,128)S(1)} %copy-done.5, bf16[3,3,128,128]{3,2,1,0:T(8,128)(2,1)S(1)} %copy-done.3, bf16[1280,384]{1,0:T(8,128)(2,1)S(1)} %copy-done.1), custom_call_target="tpu_custom_call" | custom-call | tf_op jit(solution)/shard_map/pallas_call | solution.py:224
  50.1 0.0 copy-start
  50.1 2.1 %copy-done = bf16[4,4,3,3,128,128]{5,4,3,2,1,0:T(8,128)(2,1)} copy-done((bf16[4,4,3,3,128,128]{5,4,3,2,1,0:T(8,128)(2,1)}, bf16[4,4,3,3,128,128]{5,4,3,2,1,0:T(8,128)(2,1)S(1)}, u32[]{:S(2)}) %copy-start) | copy-done | bytes 4718616
  52.2 0.0 copy-start.2
  52.2 1.0 %copy-done.2 = bf16[384,1280]{1,0:T(8,128)(2,1)} copy-done((bf16[384,1280]{1,0:T(8,128)(2,1)}, bf16[384,1280]{1,0:T(8,128)(2,1)S(1)}, u32[]{:S(2)}) %copy-start.2) | copy-done | bytes 983064
  53.3 0.0 copy-start.7
  53.3 0.5 copy-done.7
  53.8 21.3 %shard_map.65 = bf16[12,384,1024]{2,1,0:T(8,128)(2,1)} custom-call(s32[36]{0:T(128)} %copy-done.7, s32[10]{0:T(128)} %size_ref.3, bf16[4,4,3,3,128,128]{5,4,3,2,1,0:T(8,128)(2,1)} %copy-done, bf16[384,1280]{1,0:T(8,128)(2,1)} %copy-done.2, bf16[1280,1024]{1,0:T(8,128)(2,1)} %vir_ref.1), custom_call_target="tpu_custom_call" | custom-call | tf_op jit(solution)/shard_map/pallas_call | solution.py:386
Async XLA Ops:
  0.0 1.2 %copy-start.1 = (bf16[1280,384]{1,0:T(8,128)(2,1)S(1)}, bf16[1280,384]{1,0:T(8,128)(2,1)}, u32[]{:S(2)}) copy-start(bf16[1280,384]{1,0:T(8,128)(2,1)} %shard_ref.1) | copy-start | bytes 2949124
  1.2 1.0 %copy-start.3 = (bf16[3,3,128,128]{3,2,1,0:T(8,128)(2,1)S(1)}, bf16[3,3,128,128]{3,2,1,0:T(8,128)(2,1)}, u32[]{:S(2)}) copy-start(bf16[3,3,128,128]{3,2,1,0:T(8,128)(2,1)} %integrals_ref.1) | copy-start | bytes 884740
  2.2 0.7 copy-start.4
  2.9 0.7 copy-start.5
  3.6 0.7 copy-start.6
  50.1 2.1 %copy-start = (bf16[4,4,3,3,128,128]{5,4,3,2,1,0:T(8,128)(2,1)}, bf16[4,4,3,3,128,128]{5,4,3,2,1,0:T(8,128)(2,1)S(1)}, u32[]{:S(2)}) copy-start(bf16[4,4,3,3,128,128]{5,4,3,2,1,0:T(8,128)(2,1)S(1)} %get-tuple-element.9.integrals_ref) | copy-start | bytes 14155780
  52.2 1.0 %copy-start.2 = (bf16[384,1280]{1,0:T(8,128)(2,1)}, bf16[384,1280]{1,0:T(8,128)(2,1)S(1)}, u32[]{:S(2)}) copy-start(bf16[384,1280]{1,0:T(8,128)(2,1)S(1)} %get-tuple-element.10.panel_ref) | copy-start | bytes 2949124
  53.3 0.5 copy-start.7

commit v4 on v3

--- a/solution.py
+++ b/solution.py
@@ -253,7 +253,7 @@
             pltpu.SemaphoreType.DMA,
         ],
         compiler_params=pltpu.CompilerParams(
-            collective_id=0, has_side_effects=True, vmem_limit_bytes=24 * 2**20
+            collective_id=0, has_side_effects=True, vmem_limit_bytes=56 * 2**20
         ),
     )(shell_size, mask, owner, integrals, shard)
 

time: 75.9 us -> 73.6 us (0.970)
  local copies, waits for them, and re-layouts: 7.88 us -> 0 us
  Pallas kernels: 67.2 us -> 72.2 us
    unnamed x16 -> x0, local copies, waits for them, and re-layouts: 7.88 us -> none
    pallas_call x1, Pallas kernels: 21.3 us -> 24.8 us  [transform(): pl.pallas_call(transform_kernel, out_shape=jax.ShapeDtypeStruct((n_occ *...]
    pallas_call x1, Pallas kernels: 45.9 us -> 47.5 us  [gather(): pl.pallas_call(functools.partial(gather_kernel, n_pair, n_occ), out_shape...]
where the time goes in v4:
time: 73.6 us; the launch traced here: 72.2 us
  Pallas kernels  72.2 us (98%)
    pallas_call x1, Pallas kernels, gather(): pl.pallas_call(functools.partial(gather_kernel, n_pair, n_occ), out_shape...  47.5 us
    pallas_call x1, Pallas kernels, transform(): pl.pallas_call(transform_kernel, out_shape=jax.ShapeDtypeStruct((n_occ *...  24.8 us

profile of v4, /device:TPU:29, one launch (start us, length us, event | category | flops | bytes accessed | tf_op | source)
XLA Modules:
  0.0 72.2 jit_solution(3124480585177730243)
XLA Ops:
  0.0 47.5 %shard_map.64 = (bf16[4,4,3,3,128,128]{5,4,3,2,1,0:T(8,128)(2,1)}, bf16[384,1280]{1,0:T(8,128)(2,1)}, s32[36]{0:T(128)}) custom-call(s32[10]{0:T(128)} %size_ref.3, s32[10,10]{1,0:T(8,128)} %mask_ref.1, s32[10,10]{1,0:T(8,128)} %owner_ref.1, bf16[3,3,128,128]{3,2,1,0:T(8,128)(2,1)} %integrals_ref.1, bf16[1280,384]{1,0:T(8,128)(2,1)} %shard_ref.1), custom_call_target="tpu_custom_call" | custom-call | tf_op jit(solution)/shard_map/pallas_call | solution.py:224
  47.5 24.8 %shard_map.65 = bf16[12,384,1024]{2,1,0:T(8,128)(2,1)} custom-call(s32[36]{0:T(128)} %get-tuple-element.8.slots_ref, s32[10]{0:T(128)} %size_ref.3, bf16[4,4,3,3,128,128]{5,4,3,2,1,0:T(8,128)(2,1)} %get-tuple-element.9.integrals_ref, bf16[384,1280]{1,0:T(8,128)(2,1)} %get-tuple-element.10.panel_ref, bf16[1280,1024]{1,0:T(8,128)(2,1)} %vir_ref.1), custom_call_target="tpu_custom_call" | custom-call | tf_op jit(solution)/shard_map/pallas_call | solution.py:386
